TPU v7x, 512 devices: a whole 4x4x16 slice. The times are simulated.
512 devices in a mesh: gx: 32 (over y_hi, z), gy: 4 (over x), gz: 4 (over y_lo, core).
Axes of the slice: x: 4, y: 4 (y_hi: 2, y_lo: 2; y = y_hi * 2 + y_lo), z: 16, core: 2. Of those that a mesh axis runs over, the one named last changes fastest.
Arguments:
- fields: float32 [12, 256, 32, 512], P(None, 'gx', 'gy', 'gz'), as said below
- reacting: int32 [256, 32, 512], P('gx', 'gy', 'gz'), may hold values from 0 to 1, as said below
- panel_map: int32 [2, 256, 512], P(None, 'gx', 'gz'), may hold values from 0 to 4095, as said below
- layer_one: bfloat16 [1600, 12], replicated, may hold values from -4 to 4
- layer_two: bfloat16 [800, 1600], replicated, may hold values from -0.21875 to 0.21875
- layer_three: bfloat16 [400, 800], replicated, may hold values from -0.3125 to 0.3125
- layer_four: bfloat16 [12, 400], replicated, may hold values from -0.3125 to 0.3125
Outputs:
- new_fields: float32 [12, 256, 32, 512], P(None, 'gx', 'gy', 'gz')
- impulse: float32 [4096], P(('gx', 'gy', 'gz'))
Inputs may be any that keep to these rules, and one draw needn't show every extreme that they name: `fields`: component 0 (density) lies between 0.3 and 3.3; the velocities (components 1 to 3 over component 0) between -1.2 and 1.2; the pressure 0.4 (component 4 - |momentum|^2 / (2 density)) between 0.3 and 5; components 5 to 11 are 0.01 to 0.14 times component 0. Each device's aligned block of 8 x 8 x 128 cells holds at most 256 reacting cells. The blocks that share their ranges along the second and third dimensions hold exactly 64 reacting cells each on average, and one in eight of them, and at least one, hold exactly 256. `panel_map`: every panel is a patch of 8 x 8 cells of one wall, shifted by 4 cells along the first dimension and closed around it; panels are numbered in a random order and each number is used once.
All inputs are finite; a program needn't handle non-finite values.
Results may differ from a plain program's by a relative error of at most 0.0014.
Values may be sent and summed in bfloat16 or wider, within the bound.
A program may use at most 64 MiB of HBM per device.

v0:
```python
import jax
import jax.numpy as jnp
from jax import lax
from jax.sharding import PartitionSpec as P

BAL = 64
COMPS = 12
PATCH = 8
HEAT_RATIO = 1.4
TIME_STEP = 0.1
CHEM_STEP = 0.25
WENO_EPS = 1e-06


def extended(array, sides, width):
    for axis, dim in sides:
        size, length = (lax.axis_size(axis), array.shape[dim])
        up = [(i, (i + 1) % size) for i in range(size - 1)]
        down = [(j, i) for i, j in up]
        last = lax.slice_in_dim(array, length - width, length, axis=dim)
        initial = lax.slice_in_dim(array, 0, width, axis=dim)
        before = lax.ppermute(last, axis, up)
        after = lax.ppermute(initial, axis, down)
        array = jnp.concatenate([before, array, after], axis=dim)
    return array


def take_slab(array_in, begin_at, length_of, flux_axis):
    return lax.slice_in_dim(array_in, begin_at, begin_at + length_of, axis=flux_axis)


def weno_face(upwind_two, upwind_one, center, downwind_one, downwind_two):
    cand_zero = (2.0 * upwind_two - 7.0 * upwind_one + 11.0 * center) / 6.0
    cand_one = (-upwind_one + 5.0 * center + 2.0 * downwind_one) / 6.0
    cand_two = (2.0 * center + 5.0 * downwind_one - downwind_two) / 6.0
    smooth_zero = (
        13.0 / 12.0 * (upwind_two - 2.0 * upwind_one + center) ** 2
        + 0.25 * (upwind_two - 4.0 * upwind_one + 3.0 * center) ** 2
    )
    smooth_one = (
        13.0 / 12.0 * (upwind_one - 2.0 * center + downwind_one) ** 2
        + 0.25 * (upwind_one - downwind_one) ** 2
    )
    smooth_two = (
        13.0 / 12.0 * (center - 2.0 * downwind_one + downwind_two) ** 2
        + 0.25 * (3.0 * center - 4.0 * downwind_one + downwind_two) ** 2
    )
    weight_zero = 0.1 / (WENO_EPS + smooth_zero) ** 2
    weight_one = 0.6 / (WENO_EPS + smooth_one) ** 2
    weight_two = 0.3 / (WENO_EPS + smooth_two) ** 2
    weight_sum = weight_zero + weight_one + weight_two
    return (weight_zero * cand_zero + weight_one * cand_one + weight_two * cand_two) / weight_sum


def to_recon(fields):
    density = fields[0]
    velocity = fields[1:4] / density[None]
    pressure = (HEAT_RATIO - 1.0) * (
        fields[4] - 0.5 * density * jnp.sum(velocity * velocity, axis=0)
    )
    fractions = fields[5:] / density[None]
    return jnp.concatenate(
        [jnp.log(density)[None], velocity, jnp.log(pressure)[None], fractions], axis=0
    )


def normal_of(normal, ndims):
    return (jnp.arange(3) == normal).reshape((3,) + (1,) * (ndims - 1))


def side_terms(recon, normal):
    density = jnp.exp(recon[0])
    velocity = recon[1:4]
    pressure = jnp.exp(recon[4])
    fractions = recon[5:]
    speed_n = velocity[normal]
    energy = pressure / (HEAT_RATIO - 1.0) + 0.5 * density * jnp.sum(velocity * velocity, axis=0)
    conserved = jnp.concatenate(
        [density[None], density[None] * velocity, energy[None], density[None] * fractions], axis=0
    )
    mass_flux = density * speed_n
    normal_mask = normal_of(normal, recon.ndim)
    momentum_flux = mass_flux[None] * velocity + jnp.where(normal_mask, pressure[None], 0.0)
    flux_terms = jnp.concatenate(
        [
            mass_flux[None],
            momentum_flux,
            ((energy + pressure) * speed_n)[None],
            mass_flux[None] * fractions,
        ],
        axis=0,
    )
    sound_speed = jnp.sqrt(HEAT_RATIO * pressure / density)
    return (
        density,
        velocity,
        pressure,
        fractions,
        energy,
        conserved,
        flux_terms,
        speed_n,
        sound_speed,
    )


def star_state(
    density, velocity, pressure, fractions, energy, speed_n, wave_speed, contact, normal_mask
):
    relative = wave_speed - speed_n
    factor = density * relative / (wave_speed - contact)
    star_velocity = jnp.where(normal_mask, contact[None], velocity)
    star_energy = energy / density + (contact - speed_n) * (
        contact + pressure / (density * relative)
    )
    return jnp.concatenate(
        [
            factor[None],
            factor[None] * star_velocity,
            (factor * star_energy)[None],
            factor[None] * fractions,
        ],
        axis=0,
    )


def hllc_flux(left_recon, right_recon, normal):
    (
        left_density,
        left_velocity,
        left_pressure,
        left_fractions,
        left_energy,
        left_cons,
        left_flux,
        left_speed,
        left_sound,
    ) = side_terms(left_recon, normal)
    (
        right_density,
        right_velocity,
        right_pressure,
        right_fractions,
        right_energy,
        right_cons,
        right_flux,
        right_speed,
        right_sound,
    ) = side_terms(right_recon, normal)
    wave_left = jnp.minimum(left_speed - left_sound, right_speed - right_sound)
    wave_right = jnp.maximum(left_speed + left_sound, right_speed + right_sound)
    left_rel = wave_left - left_speed
    right_rel = wave_right - right_speed
    contact = (
        right_pressure
        - left_pressure
        + left_density * left_speed * left_rel
        - right_density * right_speed * right_rel
    ) / (left_density * left_rel - right_density * right_rel)
    normal_mask = normal_of(normal, left_recon.ndim)
    star_left = star_state(
        left_density,
        left_velocity,
        left_pressure,
        left_fractions,
        left_energy,
        left_speed,
        wave_left,
        contact,
        normal_mask,
    )
    star_right = star_state(
        right_density,
        right_velocity,
        right_pressure,
        right_fractions,
        right_energy,
        right_speed,
        wave_right,
        contact,
        normal_mask,
    )
    left_star_flux = left_flux + wave_left[None] * (star_left - left_cons)
    right_star_flux = right_flux + wave_right[None] * (star_right - right_cons)
    return jnp.where(
        wave_left[None] >= 0,
        left_flux,
        jnp.where(
            contact[None] >= 0,
            left_star_flux,
            jnp.where(wave_right[None] > 0, right_star_flux, right_flux),
        ),
    )


def face_flux(padded, normal):
    flux_axis = normal + 1
    face_count = padded.shape[flux_axis] - 5
    stencil = [take_slab(padded, offset, face_count, flux_axis) for offset in range(6)]
    left_state = weno_face(stencil[0], stencil[1], stencil[2], stencil[3], stencil[4])
    right_state = weno_face(stencil[5], stencil[4], stencil[3], stencil[2], stencil[1])
    return hllc_flux(left_state, right_state, normal)


def mirror_walls(padded, normal, at_first, at_last):
    flux_axis = normal + 1
    cell_count = padded.shape[flux_axis] - 6
    flip_sign = (
        jnp.where(jnp.arange(padded.shape[0]) == 1 + normal, -1.0, 1.0)
        .astype(padded.dtype)
        .reshape((-1, 1, 1, 1))
    )
    ghost_low = jnp.flip(take_slab(padded, 3, 3, flux_axis), flux_axis) * flip_sign
    ghost_high = jnp.flip(take_slab(padded, cell_count, 3, flux_axis), flux_axis) * flip_sign
    low_side = jnp.where(at_first, ghost_low, take_slab(padded, 0, 3, flux_axis))
    high_side = jnp.where(at_last, ghost_high, take_slab(padded, cell_count + 3, 3, flux_axis))
    return jnp.concatenate(
        [low_side, take_slab(padded, 3, cell_count, flux_axis), high_side], axis=flux_axis
    )


def chem_rates(features, layer_one, layer_two, layer_three, layer_four):
    hidden_one = jax.nn.gelu(
        jnp.dot(layer_one, features, preferred_element_type=jnp.float32)
    ).astype(jnp.bfloat16)
    hidden_two = jax.nn.gelu(
        jnp.dot(layer_two, hidden_one, preferred_element_type=jnp.float32)
    ).astype(jnp.bfloat16)
    hidden_three = jax.nn.gelu(
        jnp.dot(layer_three, hidden_two, preferred_element_type=jnp.float32)
    ).astype(jnp.bfloat16)
    return jnp.dot(layer_four, hidden_three, preferred_element_type=jnp.float32).astype(
        jnp.bfloat16
    )


def body(fields, reacting, panel_map, layer_one, layer_two, layer_three, layer_four):
    recon_fields = to_recon(fields)
    gx_count = lax.axis_size("gx")
    gy_count = lax.axis_size("gy")
    gz_count = lax.axis_size("gz")
    at_first = (lax.axis_index("gx") == 0, lax.axis_index("gy") == 0, lax.axis_index("gz") == 0)
    at_last = (
        lax.axis_index("gx") == gx_count - 1,
        lax.axis_index("gy") == gy_count - 1,
        lax.axis_index("gz") == gz_count - 1,
    )
    padded = extended(recon_fields, (("gx", 1), ("gy", 2), ("gz", 3)), 3)
    line_fields = (padded[:, :, 3:-3, 3:-3], padded[:, 3:-3, :, 3:-3], padded[:, 3:-3, 3:-3, :])
    update = jnp.zeros_like(fields)
    push_low = None
    push_high = None
    for normal in range(3):
        line_block = mirror_walls(line_fields[normal], normal, at_first[normal], at_last[normal])
        face_fluxes = face_flux(line_block, normal)
        cell_count = face_fluxes.shape[normal + 1] - 1
        change = take_slab(face_fluxes, 1, cell_count, normal + 1) - take_slab(
            face_fluxes, 0, cell_count, normal + 1
        )
        update = update + change
        if normal == 1:
            push_low = face_fluxes[2, :, 0, :]
            push_high = face_fluxes[2, :, cell_count, :]
    cell_total = reacting.size
    react_flags = reacting.reshape(cell_total)
    capacity = BAL * min(4, gx_count)
    per_peer = capacity // gx_count
    row_rank = jnp.cumsum(react_flags) - 1
    slot_index = jnp.where(
        react_flags == 1, row_rank % gx_count * per_peer + row_rank // gx_count, capacity
    )
    flat_features = recon_fields.reshape(COMPS, cell_total).astype(jnp.bfloat16)
    packed = (
        jnp.zeros((COMPS, capacity), jnp.bfloat16).at[:, slot_index].set(flat_features, mode="drop")
    )
    rate_packed = chem_rates(packed, layer_one, layer_two, layer_three, layer_four)
    gathered = rate_packed[:, jnp.where(react_flags == 1, slot_index, 0)]
    source = jnp.where(react_flags[None, :] == 1, gathered.astype(jnp.float32), 0.0).reshape(
        fields.shape
    )
    new_fields = fields - TIME_STEP * update + CHEM_STEP * source
    on_low = lax.axis_index("gy") == 0
    on_high = lax.axis_index("gy") == gy_count - 1
    push_values = jnp.concatenate(
        [
            jnp.where(on_low, push_low, 0.0).reshape(-1),
            jnp.where(on_high, push_high, 0.0).reshape(-1),
        ]
    )
    panel_ids = jnp.concatenate([panel_map[0].reshape(-1), panel_map[1].reshape(-1)])
    panels_all = 2 * (fields.shape[1] * gx_count // PATCH) * (fields.shape[3] * gz_count // PATCH)
    own_panels = panels_all // (gx_count * gy_count * gz_count)
    partial_loads = jax.ops.segment_sum(push_values, panel_ids, num_segments=panels_all)
    totals = lax.psum(partial_loads, ("gx", "gy", "gz"))
    flat_index = (
        lax.axis_index("gx") * gy_count + lax.axis_index("gy")
    ) * gz_count + lax.axis_index("gz")
    result = lax.dynamic_slice_in_dim(totals, flat_index * own_panels, own_panels)
    impulse = result / float(PATCH * PATCH)
    return (new_fields, impulse)


def solution(mesh):
    return jax.shard_map(
        body,
        mesh=mesh,
        in_specs=(
            P(None, "gx", "gy", "gz"),
            P("gx", "gy", "gz"),
            P(None, "gx", "gz"),
            P(),
            P(),
            P(),
            P(),
        ),
        out_specs=(P(None, "gx", "gy", "gz"), P(("gx", "gy", "gz"))),
        check_vma=False,
    )
```

profile of v0, /device:TPU:1, one launch (start us, length us, event | category | flops | bytes accessed | tf_op | source)
XLA Modules:
  0.0 275.4 jit_solution(14904916895954684997)
XLA Ops:
  5.1 5.0 %collective-permute-start = (f32[12,3,8,128]{3,2,1,0:T(8,128)}, f32[12,3,8,128]{3,2,1,0:T(8,128)}, u32[]{:S(2)}, u32[]{:S(2)}) collective-permute-start(f32[12,3,8,128]{3,2,1,0:T(8,128)} %get-tuple-element.138), channel_id=1, source_target_pairs={{0,16},{16,32},{32,48},{48,64},{64,80},{80,96},{96,112},{112,128},... | collective-permute-start | bytes 442376 | tf_op jit(solution)/shard_map/ppermute | solution.py:22
  10.2 1.3 collective-permute-start.1
  16.4 2.7 copy.63
  21.6 21.7 %scatter_custom_fusion = bf16[12,256]{0,1:T(8,128)(2,1)} fusion(s32[8192]{0:T(1024)S(1)} %bitcast.214, bf16[8192,12]{1,0:T(8,128)(2,1)} %copy.63, bf16[]{:T(256)} %constant.78.clone.1), kind=kCustom, calls=%fused_computation.316 | custom fusion | bytes 6656 | tf_op jit(solution)/shard_map/scatter | solution.py:274
  43.3 3.2 %fusion.16 = bf16[800,256]{1,0:T(8,128)(2,1)} fusion(bf16[800,1600]{1,0:T(8,128)(2,1)S(1)} %copy-done, bf16[12,256]{0,1:T(8,128)(2,1)} %scatter_custom_fusion, bf16[1600,12]{0,1:T(8,128)(2,1)} %param.10), kind=kOutput, calls=%fused_computation.28 | convolution fusion | flops 670720000 | bytes 3014144 | tf_op jit(solution)/shard_map/dot_general | solution.py:227
  46.5 1.8 fusion.8
  48.8 1.8 rev.23
  50.6 1.8 rev.24
  52.4 1.9 rev.25
  55.4 29.4 %gather_fusion = bf16[8192,12]{1,0:T(8,128)(2,1)} fusion(bf16[12,256]{0,1:T(8,128)(2,1)S(1)} %copy.64, s32[8192]{0:T(1024)S(1)} %broadcast_clamp_fusion), kind=kCustom, calls=%fused_computation | custom fusion | bytes 425984 | tf_op jit(solution)/shard_map/gather | solution.py:277
  84.8 3.8 %convert_element_type.31 = f32[8192,12]{1,0:T(8,128)} convert(bf16[8192,12]{1,0:T(8,128)(2,1)} %gather_fusion) | non-fusion elementwise | flops 98304 | bytes 589824 | tf_op jit(solution)/shard_map/convert_element_type | solution.py:278
  88.6 3.6 %copy.66 = f32[12,8,8,128]{3,2,1,0:T(8,128)} copy(f32[12,8,8,128]{0,3,2,1:T(8,128)} %bitcast.175) | data formatting | bytes 786432 | tf_op jit(solution)/shard_map/convert_element_type | solution.py:278
  94.0 1.9 add_divide_fusion.2
  97.2 3.1 %collective-permute-start.2 = (f32[12,14,3,128]{3,1,2,0:T(8,128)S(1)}, f32[12,14,3,128]{3,1,2,0:T(8,128)S(1)}, u32[]{:S(2)}, u32[]{:S(2)}) collective-permute-start(f32[12,14,3,128]{3,1,2,0:T(8,128)S(1)} %copy.53), channel_id=1, source_target_pairs={{0,4},{4,8},{8,12},{1,5},{5,9},{9,13},{2,6},{6,10},{10,14},{3,7},{... | collective-permute-start | bytes 774152 | tf_op jit(solution)/shard_map/ppermute | solution.py:22
  100.4 1.5 collective-permute-start.3
  103.0 1.9 collective-permute-done.2
  105.1 3.7 %collective-permute-done.3 = f32[12,14,3,128]{3,1,2,0:T(8,128)S(1)} collective-permute-done((f32[12,14,3,128]{3,1,2,0:T(8,128)S(1)}, f32[12,14,3,128]{3,1,2,0:T(8,128)S(1)}, u32[]{:S(2)}, u32[]{:S(2)}) %collective-permute-start.3) | collective-permute-done | bytes 258080 | tf_op jit(solution)/shard_map/ppermute | solution.py:23
  109.9 3.6 %add_divide_fusion.1 = (f32[12,8,9,128]{3,2,1,0:T(8,128)S(1)}, f32[12,8,9,128]{3,2,1,0:T(8,128)S(1)}) fusion(f32[12,8,11,128]{3,2,1,0:T(8,128)S(1)} %get-tuple-element.130, f32[12,8,11,128]{3,2,1,0:T(8,128)S(1)} %get-tuple-element.131), kind=kLoop, calls=%fused_computation.80 | loop fusion | flops 13713408 | bytes 3538944 | tf_op jit(solution)/shard_map/div | solution.py:52
  116.2 14.0 %scatter_custom_fusion.1 = f32[4096]{0:T(1024)S(1)} fusion(s32[2048]{0:T(1024)} %pad_add_fusion, f32[2048]{0:T(1024)S(1)} %pad_maximum_fusion.9, f32[]{:T(128)} %constant.54.clone.1), kind=kCustom, calls=%fused_computation.342 | custom fusion | flops 2048 | bytes 16896 | tf_op jit(solution)/shard_map/scatter-add | solution.py:293
  130.3 111.0 %psum.7 = f32[4096]{0:T(1024)S(1)} all-reduce(f32[4096]{0:T(1024)S(1)} %scatter_custom_fusion.1), channel_id=1, replica_groups=mesh['gx'=32,'gy'=4,'gz'=4] {'gx','gy','gz'}, use_global_device_ids=true, to_apply=%region_11.12 | all-reduce | flops 4096 | bytes 32768 | tf_op jit(solution)/shard_map/psum | solution.py:294
  241.3 1.5 pad_maximum_fusion
  242.8 2.0 fusion.169
  244.8 3.4 %copy.59 = f32[12,14,14,3]{2,1,3,0:T(8,128)} copy(f32[12,14,14,3]{3,2,1,0:T(8,128)} %get-tuple-element.58) | data formatting | bytes 56448 | tf_op jit(solution)/shard_map/slice | solution.py:20
  248.2 2.1 collective-permute-start.4
  250.3 3.4 %copy.61 = f32[12,14,14,3]{2,1,3,0:T(8,128)} copy(f32[12,14,14,3]{3,2,1,0:T(8,128)} %get-tuple-element.57) | data formatting | bytes 56448 | tf_op jit(solution)/shard_map/slice | solution.py:21
  253.7 2.9 %collective-permute-start.5 = (f32[12,14,14,3]{2,1,3,0:T(8,128)}, f32[12,14,14,3]{2,1,3,0:T(8,128)}, u32[]{:S(2)}, u32[]{:S(2)}) collective-permute-start(f32[12,14,14,3]{2,1,3,0:T(8,128)} %copy.61), channel_id=1, source_target_pairs={{1,0},{2,1},{3,2},{5,4},{6,5},{7,6},{9,8},{10,9},{11,10},{13,12},{... | collective-permute-start | bytes 84680 | tf_op jit(solution)/shard_map/ppermute | solution.py:23
  257.2 1.7 slice.418
  258.9 2.3 copy.67
  262.1 1.7 slice.424
  263.8 2.3 copy.68
  266.1 1.5 multiply_select_fusion
  267.8 3.9 %add_divide_fusion = (f32[12,8,8,129]{3,2,1,0:T(8,128)S(1)}, f32[12,8,8,129]{3,2,1,0:T(8,128)S(1)}) fusion(f32[12,8,8,131]{3,2,1,0:T(8,128)S(1)} %get-tuple-element.134, f32[12,8,8,131]{3,2,1,0:T(8,128)S(1)} %get-tuple-element.135), kind=kLoop, calls=%fused_computation.53 | loop fusion | flops 12284928 | bytes 3170304 | tf_op jit(solution)/shard_map/div | solution.py:52
  (119 shorter events, 26.8 us)
Async XLA Ops:
  0.6 42.6 %copy-start = (bf16[800,1600]{1,0:T(8,128)(2,1)S(1)}, bf16[800,1600]{1,0:T(8,128)(2,1)}, u32[]{:S(2)}) copy-start(bf16[800,1600]{1,0:T(8,128)(2,1)} %param.11) | copy-start | bytes 7680004
  4.3 11.0 %copy-start.10 = (s32[2,8,128]{2,1,0:T(8,128)S(1)}, s32[2,8,128]{2,1,0:T(8,128)}, u32[]{:S(2)}) copy-start(s32[2,8,128]{2,1,0:T(8,128)} %param.9) | copy-start | bytes 24580
  5.1 87.6 %collective-permute-start = (f32[12,3,8,128]{3,2,1,0:T(8,128)}, f32[12,3,8,128]{3,2,1,0:T(8,128)}, u32[]{:S(2)}, u32[]{:S(2)}) collective-permute-start(f32[12,3,8,128]{3,2,1,0:T(8,128)} %get-tuple-element.138), channel_id=1, source_target_pairs={{0,16},{16,32},{32,48},{48,64},{64,80},{80,96},{96,112},{112,128},... | collective-permute-start | bytes 442376 | tf_op jit(solution)/shard_map/ppermute | solution.py:22
  10.2 82.6 %collective-permute-start.1 = (f32[12,3,8,128]{3,2,1,0:T(8,128)}, f32[12,3,8,128]{3,2,1,0:T(8,128)}, u32[]{:S(2)}, u32[]{:S(2)}) collective-permute-start(f32[12,3,8,128]{3,2,1,0:T(8,128)} %get-tuple-element.139), channel_id=1, source_target_pairs={{16,0},{32,16},{48,32},{64,48},{80,64},{96,80},{112,96},{128,112},... | collective-permute-start | bytes 442376 | tf_op jit(solution)/shard_map/ppermute | solution.py:23
  15.3 3.8 %copy-start.9 = (s32[8,8,128]{2,1,0:T(8,128)S(1)}, s32[8,8,128]{2,1,0:T(8,128)}, u32[]{:S(2)}) copy-start(s32[8,8,128]{2,1,0:T(8,128)} %param.8) | copy-start | bytes 98308
  43.3 3.2 %copy-start.16 = (bf16[12,400]{1,0:T(8,128)(2,1)S(1)}, bf16[12,400]{1,0:T(8,128)(2,1)}, u32[]{:S(2)}) copy-start(bf16[12,400]{1,0:T(8,128)(2,1)} %param.13) | copy-start | bytes 28804
  88.6 4.2 %copy-start.15 = (f32[12]{0:T(128)S(1)}, f32[12]{0:T(128)}, u32[]{:S(2)}) copy-start(f32[12]{0:T(128)} %compare_select_fusion.7) | copy-start | bytes 148
  97.2 7.7 %collective-permute-start.2 = (f32[12,14,3,128]{3,1,2,0:T(8,128)S(1)}, f32[12,14,3,128]{3,1,2,0:T(8,128)S(1)}, u32[]{:S(2)}, u32[]{:S(2)}) collective-permute-start(f32[12,14,3,128]{3,1,2,0:T(8,128)S(1)} %copy.53), channel_id=1, source_target_pairs={{0,4},{4,8},{8,12},{1,5},{5,9},{9,13},{2,6},{6,10},{10,14},{3,7},{... | collective-permute-start | bytes 774152 | tf_op jit(solution)/shard_map/ppermute | solution.py:22
  100.4 8.4 %collective-permute-start.3 = (f32[12,14,3,128]{3,1,2,0:T(8,128)S(1)}, f32[12,14,3,128]{3,1,2,0:T(8,128)S(1)}, u32[]{:S(2)}, u32[]{:S(2)}) collective-permute-start(f32[12,14,3,128]{3,1,2,0:T(8,128)S(1)} %copy.55), channel_id=1, source_target_pairs={{4,0},{8,4},{12,8},{5,1},{9,5},{13,9},{6,2},{10,6},{14,10},{7,3},{... | collective-permute-start | bytes 774152 | tf_op jit(solution)/shard_map/ppermute | solution.py:23
  102.0 0.7 copy-start.14
  102.7 6.2 %copy-start.7 = (f32[12,8,3,128]{3,2,1,0:T(4,128)S(1)}, f32[12,8,3,128]{3,2,1,0:T(4,128)}, u32[]{:S(2)}) copy-start(f32[12,8,3,128]{3,2,1,0:T(4,128)} %rev.23) | copy-start | bytes 442372
  102.7 6.2 %copy-start.8 = (f32[12,8,3,128]{3,2,1,0:T(4,128)S(1)}, f32[12,8,3,128]{3,2,1,0:T(4,128)}, u32[]{:S(2)}) copy-start(f32[12,8,3,128]{3,2,1,0:T(4,128)} %rev.24) | copy-start | bytes 442372
  105.0 4.1 %copy-start.3 = (f32[12,14,3,128]{3,2,1,0:T(4,128)}, f32[12,14,3,128]{3,2,1,0:T(4,128)S(1)}, u32[]{:S(2)}) copy-start(f32[12,14,3,128]{3,2,1,0:T(4,128)S(1)} %copy.54) | copy-start | bytes 774148
  109.0 0.7 copy-start.4
  114.0 0.7 copy-start.13
  115.3 0.9 copy-start.1
  248.2 9.0 %collective-permute-start.4 = (f32[12,14,14,3]{2,1,3,0:T(8,128)}, f32[12,14,14,3]{2,1,3,0:T(8,128)}, u32[]{:S(2)}, u32[]{:S(2)}) collective-permute-start(f32[12,14,14,3]{2,1,3,0:T(8,128)} %copy.59), channel_id=1, source_target_pairs={{0,1},{1,2},{2,3},{4,5},{5,6},{6,7},{8,9},{9,10},{10,11},{12,13},{... | collective-permute-start | bytes 84680 | tf_op jit(solution)/shard_map/ppermute | solution.py:22
  250.3 15.7 %copy-start.12 = (f32[12]{0:T(128)S(1)}, f32[12]{0:T(128)}, u32[]{:S(2)}) copy-start(f32[12]{0:T(128)} %compare_select_fusion.5) | copy-start | bytes 148
  253.7 8.3 %collective-permute-start.5 = (f32[12,14,14,3]{2,1,3,0:T(8,128)}, f32[12,14,14,3]{2,1,3,0:T(8,128)}, u32[]{:S(2)}, u32[]{:S(2)}) collective-permute-start(f32[12,14,14,3]{2,1,3,0:T(8,128)} %copy.61), channel_id=1, source_target_pairs={{1,0},{2,1},{3,2},{5,4},{6,5},{7,6},{9,8},{10,9},{11,10},{13,12},{... | collective-permute-start | bytes 84680 | tf_op jit(solution)/shard_map/ppermute | solution.py:23
  272.3 0.7 copy-start.11
  273.1 1.1 copy-start.2
  273.1 1.2 copy-start.5
  273.1 1.3 copy-start.6
where the time goes:
time: 276 us; the launch traced here: 275 us
  blocking collectives  111 us (40%)
  local copies, waits for them, and re-layouts  87.9 us (32%)
  other arithmetic  47.9 us (17%)
  starting transfers between devices  15.9 us (6%)
  waiting for transfers between devices  6.54 us (2%)
  matrix products  4.97 us (2%)
    psum x1, blocking collectives, body(): totals = lax.psum(partial_loads, ('gx', 'gy', 'gz'))  111 us
    gather x1, local copies, waits for them, and re-layouts, body(): gathered = rate_packed[:, jnp.where(react_flags == 1, slot_index, 0)]  29.4 us
    scatter x1, local copies, waits for them, and re-layouts, body(): jnp.zeros((COMPS, capacity), jnp.bfloat16).at[:, slot_index]  21.7 us
    scatter-add x1, other arithmetic, body(): jax.ops.segment_sum(push_values, panel_ids, num_segments=panels_all)  14 us
    ppermute x3, starting transfers between devices, extended(): before = lax.ppermute(last, axis, up)  10.3 us
    div x3, other arithmetic, weno_face(): (weight_zero * cand_zero + weight_one * cand_one + weight_two * cand_two)...  9.43 us
    unnamed x38, local copies, waits for them, and re-layouts  7.97 us
    ppermute x3, starting transfers between devices, extended(): after = lax.ppermute(initial, axis, down)  5.61 us
  transfers between devices with their start and end apart: 6, of which 3 were waited for; matrix products, arithmetic and copies ran while one was open for 33% of the time, Pallas kernels for 0%

commit v1 on v0

--- a/solution.py
+++ b/solution.py
@@ -291,7 +291,7 @@
     panels_all = 2 * (fields.shape[1] * gx_count // PATCH) * (fields.shape[3] * gz_count // PATCH)
     own_panels = panels_all // (gx_count * gy_count * gz_count)
     partial_loads = jax.ops.segment_sum(push_values, panel_ids, num_segments=panels_all)
-    totals = lax.psum(partial_loads, ("gx", "gy", "gz"))
+    totals = jnp.sum(lax.all_gather(partial_loads, ("gx", "gy", "gz")), axis=0)
     flat_index = (
         lax.axis_index("gx") * gy_count + lax.axis_index("gy")
     ) * gz_count + lax.axis_index("gz")

time: 276 us -> 914 us (3.31)
  waiting for transfers between devices: 6.54 us -> 722 us
  blocking collectives: 111 us -> 0 us
  between operations: 1.23 us -> 14.8 us
    all_gather x0 -> x1, waiting for transfers between devices: none -> 721 us  [body(): totals = jnp.sum(lax.all_gather(partial_loads, ('gx', 'gy', 'gz')), axis=0)]
    psum x1 -> x0, blocking collectives: 111 us -> none  [body(): totals = lax.psum(partial_loads, ('gx', 'gy', 'gz'))]
    all_gather x0 -> x1, local copies, waits for them, and re-layouts: none -> 9.36 us  [body(): totals = jnp.sum(lax.all_gather(partial_loads, ('gx', 'gy', 'gz')), axis=0)]
  transfers between devices with their start and end apart: 6 -> 7, of which waited for: 3 -> 3; matrix products, arithmetic and copies ran while one was open for 33% -> 11% of each run, Pallas kernels for 0% -> 0%
where the time goes in v1:
time: 914 us; the launch traced here: 908 us
  waiting for transfers between devices  722 us (79%)
  local copies, waits for them, and re-layouts  90.7 us (10%)
  other arithmetic  52.3 us (6%)
  starting transfers between devices  23.4 us (3%)
  between operations  14.8 us (2%)
    all_gather x1, waiting for transfers between devices, body(): totals = jnp.sum(lax.all_gather(partial_loads, ('gx', 'gy', 'gz')), axis=0)  721 us
    gather x1, local copies, waits for them, and re-layouts, body(): gathered = rate_packed[:, jnp.where(react_flags == 1, slot_index, 0)]  24 us
    scatter x1, local copies, waits for them, and re-layouts, body(): jnp.zeros((COMPS, capacity), jnp.bfloat16).at[:, slot_index]  21.7 us
  transfers between devices with their start and end apart: 7, of which 3 were waited for; matrix products, arithmetic and copies ran while one was open for 11% of the time, Pallas kernels for 0%

profile of v1, /device:TPU:1, one launch (start us, length us, event | category | flops | bytes accessed | tf_op | source)
XLA Modules:
  0.0 908.0 jit_solution(2373488764508664838)
XLA Ops:
  7.2 1.5 convert_bitcast_fusion.3
  8.8 1.6 convert_bitcast_fusion
  11.3 1.4 convert_bitcast_fusion.2
  12.8 1.3 collective-permute-start.1
  14.1 5.0 collective-permute-start
  23.1 1.3 collective-permute-start.3
  25.2 4.7 collective-permute-start.2
  29.9 1.9 rev.26
  32.7 1.8 rev.24
  34.5 1.8 rev.23
  38.5 1.3 slice_select_fusion
  40.1 3.6 add_divide_fusion.1
  46.1 14.5 %scatter_custom_fusion.1 = f32[4096]{0:T(1024)} fusion(s32[2048]{0:T(1024)S(1)} %pad_add_fusion, f32[2048]{0:T(1024)S(1)} %pad_maximum_fusion.9, f32[]{:T(128)} %constant.54.clone.1), kind=kCustom, calls=%fused_computation.342 | custom fusion | flops 2048 | bytes 16388 | tf_op jit(solution)/shard_map/scatter-add | solution.py:293
  65.1 2.7 copy.81
  69.8 21.7 %scatter_custom_fusion = bf16[12,256]{0,1:T(8,128)(2,1)} fusion(s32[8192]{0:T(1024)S(1)} %bitcast.214, bf16[8192,12]{1,0:T(8,128)(2,1)} %copy.81, bf16[]{:T(256)} %constant.78.clone.1), kind=kCustom, calls=%fused_computation.316 | custom fusion | bytes 6656 | tf_op jit(solution)/shard_map/scatter | solution.py:274
  91.5 3.2 fusion.16
  94.7 1.8 fusion.8
  96.7 24.0 %gather_fusion = bf16[8192,12]{1,0:T(8,128)(2,1)S(1)} fusion(bf16[12,256]{0,1:T(8,128)(2,1)S(1)} %copy.82, s32[8192]{0:T(1024)S(1)} %broadcast_clamp_fusion), kind=kCustom, calls=%fused_computation | custom fusion | bytes 425984 | tf_op jit(solution)/shard_map/gather | solution.py:277
  120.7 2.3 convert_element_type.31
  123.0 3.6 copy.84
  126.9 1.9 add_divide_fusion.2
  132.6 1.1 slice_multiply_fusion.12
  134.0 2.0 fusion.169
  136.1 3.5 copy.79
  139.6 9.0 collective-permute-start.5
  148.6 2.1 copy.77
  150.7 2.1 collective-permute-start.4
  152.9 1.7 fusion.76
  158.7 3.9 add_divide_fusion
  165.9 721.4 %all-gather.3.cloned.1.call-done = f32[2097152]{0:T(1024)} async-done(((f32[4096]{0:T(1024)}), f32[2097152]{0:T(1024)}) %all-gather.3.cloned.1.call-update) | async-done | bytes 8388624 | tf_op jit(solution)/shard_map/all_gather | solution.py:294
  887.3 9.4 %reshape.288 = f32[512,4096]{1,0:T(8,128)} reshape(f32[2097152]{0:T(1024)} %all-gather.3.cloned.1.call-done) | data formatting | bytes 16777216 | tf_op jit(solution)/shard_map/all_gather | solution.py:294
  896.7 3.9 reduce_sum.100
  (165 shorter events, 30.2 us)
Async XLA Ops:
  7.2 84.4 %copy-start = (bf16[800,1600]{1,0:T(8,128)(2,1)S(1)}, bf16[800,1600]{1,0:T(8,128)(2,1)}, u32[]{:S(2)}) copy-start(bf16[800,1600]{1,0:T(8,128)(2,1)} %param.11) | copy-start | bytes 7680004
  7.2 880.1 %all-gather.3.cloned.1.call-start = ((), (), s32[]{:S(2)}) async-start(), calls=%async_computation | async-start | bytes 8404992 | tf_op jit(solution)/shard_map/all_gather | solution.py:294
  12.7 8.2 copy-start.36
  12.8 8.2 copy-start.19
  12.8 8.2 copy-start.21
  12.8 8.1 collective-permute-start.1
  14.1 7.1 collective-permute-start
  23.1 13.2 %collective-permute-start.3 = (f32[12,14,3,128]{3,1,2,0:T(8,128)}, f32[12,14,3,128]{3,1,2,0:T(8,128)}, u32[]{:S(2)}, u32[]{:S(2)}) collective-permute-start(f32[12,14,3,128]{3,1,2,0:T(8,128)} %copy.73), channel_id=1, source_target_pairs={{4,0},{8,4},{12,8},{5,1},{9,5},{13,9},{6,2},{10,6},{14,10},{7,3},{... | collective-permute-start | bytes 774152 | tf_op jit(solution)/shard_map/ppermute | solution.py:23
  25.2 12.2 %collective-permute-start.2 = (f32[12,14,3,128]{3,1,2,0:T(8,128)}, f32[12,14,3,128]{3,1,2,0:T(8,128)}, u32[]{:S(2)}, u32[]{:S(2)}) collective-permute-start(f32[12,14,3,128]{3,1,2,0:T(8,128)} %copy.71), channel_id=1, source_target_pairs={{0,4},{4,8},{8,12},{1,5},{5,9},{9,13},{2,6},{6,10},{10,14},{3,7},{... | collective-permute-start | bytes 774152 | tf_op jit(solution)/shard_map/ppermute | solution.py:22
  44.7 15.9 %copy-start.34 = (s32[8,8,128]{2,1,0:T(8,128)S(1)}, s32[8,8,128]{2,1,0:T(8,128)}, u32[]{:S(2)}) copy-start(s32[8,8,128]{2,1,0:T(8,128)} %param.8) | copy-start | bytes 98308
  123.0 3.7 copy-start.12
  123.0 3.7 copy-start.14
  123.0 3.7 copy-start.20
  123.0 3.7 copy-start.22
  129.0 4.7 copy-start.23
  129.0 4.7 copy-start.25
  136.0 12.6 %copy-start.2 = (f32[12,14,14,3]{3,2,1,0:T(8,128)S(1)}, f32[12,14,14,3]{3,2,1,0:T(8,128)}, u32[]{:S(2)}) copy-start(f32[12,14,14,3]{3,2,1,0:T(8,128)} %get-tuple-element.60) | copy-start | bytes 84676
  136.0 16.8 %copy-start.15 = (f32[7,9,8,128]{3,2,1,0:T(8,128)S(1)}, f32[7,9,8,128]{3,2,1,0:T(8,128)}, u32[]{:S(2)}) copy-start(f32[7,9,8,128]{3,2,1,0:T(8,128)} %get-tuple-element.116) | copy-start | bytes 774148
  136.0 16.8 %copy-start.16 = (f32[7,9,8,128]{3,2,1,0:T(8,128)S(1)}, f32[7,9,8,128]{3,2,1,0:T(8,128)}, u32[]{:S(2)}) copy-start(f32[7,9,8,128]{3,2,1,0:T(8,128)} %get-tuple-element.117) | copy-start | bytes 774148
  136.0 16.8 %copy-start.17 = (f32[7,9,8,128]{3,2,1,0:T(8,128)S(1)}, f32[7,9,8,128]{3,2,1,0:T(8,128)}, u32[]{:S(2)}) copy-start(f32[7,9,8,128]{3,2,1,0:T(8,128)} %get-tuple-element.118) | copy-start | bytes 774148
  136.0 16.8 %copy-start.18 = (f32[7,9,8,128]{3,2,1,0:T(8,128)S(1)}, f32[7,9,8,128]{3,2,1,0:T(8,128)}, u32[]{:S(2)}) copy-start(f32[7,9,8,128]{3,2,1,0:T(8,128)} %get-tuple-element.174) | copy-start | bytes 774148
  136.0 16.8 %copy-start.24 = (f32[1,9,8,128]{3,2,1,0:T(8,128)S(1)}, f32[1,9,8,128]{3,2,1,0:T(8,128)}, u32[]{:S(2)}) copy-start(f32[1,9,8,128]{3,2,1,0:T(8,128)} %copy-done.23) | copy-start | bytes 110596
  136.0 16.8 %copy-start.26 = (f32[1,9,8,128]{3,2,1,0:T(8,128)S(1)}, f32[1,9,8,128]{3,2,1,0:T(8,128)}, u32[]{:S(2)}) copy-start(f32[1,9,8,128]{3,2,1,0:T(8,128)} %copy-done.25) | copy-start | bytes 110596
  136.0 16.8 %copy-start.28 = (f32[1,9,8,128]{3,2,1,0:T(8,128)S(1)}, f32[1,9,8,128]{3,2,1,0:T(8,128)}, u32[]{:S(2)}) copy-start(f32[1,9,8,128]{3,2,1,0:T(8,128)} %copy-done.27) | copy-start | bytes 110596
  136.0 16.8 %copy-start.30 = (f32[1,9,8,128]{3,2,1,0:T(8,128)S(1)}, f32[1,9,8,128]{3,2,1,0:T(8,128)}, u32[]{:S(2)}) copy-start(f32[1,9,8,128]{3,2,1,0:T(8,128)} %copy-done.29) | copy-start | bytes 110596
  136.1 16.8 %copy-start.32 = (f32[1,9,8,128]{3,2,1,0:T(8,128)S(1)}, f32[1,9,8,128]{3,2,1,0:T(8,128)}, u32[]{:S(2)}) copy-start(f32[1,9,8,128]{3,2,1,0:T(8,128)} %copy-done.31) | copy-start | bytes 110596
  136.1 16.8 %copy-start.35 = (pred[9,8,128]{2,1,0:T(8,128)(4,1)S(1)}, pred[9,8,128]{2,1,0:T(8,128)(4,1)}, u32[]{:S(2)}) copy-start(pred[9,8,128]{2,1,0:T(8,128)(4,1)} %compare_bitcast_fusion.6) | copy-start | bytes 27652
  139.6 15.0 %collective-permute-start.5 = (f32[12,14,14,3]{2,1,3,0:T(8,128)}, f32[12,14,14,3]{2,1,3,0:T(8,128)}, u32[]{:S(2)}, u32[]{:S(2)}) collective-permute-start(f32[12,14,14,3]{2,1,3,0:T(8,128)} %copy.79), channel_id=1, source_target_pairs={{1,0},{2,1},{3,2},{5,4},{6,5},{7,6},{9,8},{10,9},{11,10},{13,12},{... | collective-permute-start | bytes 84680 | tf_op jit(solution)/shard_map/ppermute | solution.py:23
  150.7 5.9 collective-permute-start.4
  152.9 5.3 copy-start.9
  152.9 5.3 copy-start.10
  896.7 4.5 copy-start.1
  (13 other events, 19.6 us)
Sparse Core Ops, SparseCore 0:
  60.7 826.5 all-gather.2
